TPU v7x, 256 devices: a whole 4x4x8 slice. The times are simulated.
256 devices in a mesh: ctx: 4 (over x_lo, core), br: 64 (over x_hi, y, z).
Axes of the slice: x: 4 (x_hi: 2, x_lo: 2; x = x_hi * 2 + x_lo), y: 4, z: 8, core: 2. Of those that a mesh axis runs over, the one named last changes fastest.
Arguments:
- queries: bfloat16 [128, 8192], P('br', 'ctx'), may hold values from -80 to 80
- prefix_keys: bfloat16 [131072, 1024], P(('ctx', 'br')), may hold values from -4 to 4
- prefix_values: bfloat16 [131072, 1024], P(('ctx', 'br')), may hold values from -6 to 6
- branch_suffix_keys: bfloat16 [128, 2048, 1024], P('br', 'ctx'), may hold values from -8 to 8
- suffix_values: bfloat16 [128, 2048, 1024], P('br', 'ctx'), may hold values from -6 to 6
- lengths: int32 [128], P('br'), may hold values from 512 to 2048
Outputs:
- attended: bfloat16 [128, 8192], P('br', 'ctx')
All inputs are finite; a program needn't handle non-finite values.
Results may differ from a plain program's by a relative error of at most 0.0045.
Values may be sent and summed in bfloat16 or wider, within the bound.
A program may use at most 64 MiB of HBM per device.

v0:
```python
import functools

import jax
import jax.numpy as jnp
from jax import lax
from jax.experimental import pallas as pl
from jax.experimental.pallas import tpu as pltpu
from jax.sharding import PartitionSpec as P

MESH = pl.DeviceIdType.MESH
BF = jnp.bfloat16
F32 = jnp.float32

D = 128
SPAN = 512
NX, NY, NZ = 4, 4, 8
ROWS = 16
TILE = 144
SCALE = D ** (-0.5)
LOG2E = 1.4426950408889634
C2 = SCALE * LOG2E
NEG = -1e30
LAST = 3
FAR = (4, 3, 5, 2, 6, 1, 7)
ACROSS = (2, 1, 3)
CHUNK = 256


def nt(a, b):
    return lax.dot_general(a, b, (((1,), (1,)), ((), ())), preferred_element_type=F32)


def pack(ref, numer, top, denom):
    row = lax.broadcasted_iota(jnp.int32, (16, top.shape[1]), 0)
    high = denom.astype(BF).astype(F32)
    low = denom - high
    stats = jnp.where(row == 0, top, jnp.where(row == 1, high, low))
    ref[0:D, :] = numer.astype(BF)
    ref[D:TILE, :] = stats.astype(BF)


def merge(refs):
    stats = [r[D:TILE, :].astype(F32) for r in refs]
    tops = [s[0:1, :] for s in stats]
    top = tops[0]
    for t in tops[1:]:
        top = jnp.maximum(top, t)
    numer, denom = None, None
    for r, s, t in zip(refs, stats, tops):
        factor = jnp.exp2((t - top) * C2)
        n = r[0:D, :].astype(F32) * factor
        d = (s[1:2, :] + s[2:3, :]) * factor
        numer = n if numer is None else numer + n
        denom = d if denom is None else denom + d
    return numer, top, denom


def kernel(
    len_ref, q_ref, pk, pv, sk, sv, out_ref,
    qraw, qscr, qz, qc, q0, q1, kbuf, vbuf, vt, skb, svb, qbd, ss, ps, pad,
    o0, o1, rx0, rx1, m0, m1, ry0, ry1, zb, rz, sb, sr, fs, ft, oscr,
    sent, rz1, rq2, rq3, rp4, rp5, rp6, rctx, rsuf, rkv, loc,
):
    c = lax.axis_index("ctx")
    br = lax.axis_index("br")
    core = c % 2
    xlo = c // 2
    z = br % NZ
    y = (br // NZ) % NY
    xhi = br // (NZ * NY)
    x = xhi * 2 + xlo

    def dev(px, py, pz, pc):
        return ((px % 2) * 2 + pc, (px // 2) * (NZ * NY) + py * NZ + pz)

    def xpeer(i):
        return dev((x + i) % NX, y, z, core)

    def ypeer(i):
        return dev(x, (y + i) % NY, z, core)

    def zpeer(i):
        return dev(x, y, (z + i) % NZ, core)

    def cpeer(i):
        return ((c + i) % 4, br)

    mate = dev(x, y, z, 1 - core)

    def remote(src, dst, ssem, rsem, who):
        return pltpu.make_async_remote_copy(
            src_ref=src, dst_ref=dst, send_sem=ssem, recv_sem=rsem, device_id=who, device_id_type=MESH
        )

    def push(src, dst, phase, rsem, who):
        remote(src, dst, sent.at[phase], rsem, who).start()

    def take(sem, kib):
        size = pad.at[0 : kib // 4]
        pltpu.make_async_copy(size, size, sem).wait()

    def load(src, dst, n):
        pltpu.make_async_copy(src, dst, loc.at[n]).start()

    def cols(a, k):
        return pl.ds(pl.multiple_of((a * 2 + k) * 256, 256), 256)

    barrier = pltpu.get_barrier_semaphore()
    peers = [zpeer(i) for i in FAR] + [ypeer(i) for i in ACROSS] + [xpeer(i) for i in ACROSS]
    peers += [mate, dev(x + 1 - 2 * xlo, y, z, 1 - core)]
    for who in peers:
        pl.semaphore_signal(barrier, inc=1, device_id=who, device_id_type=MESH)

    load(q_ref, qraw, 0)
    for a in range(2):
        load(pv.at[:, cols(a, core)], vbuf.at[a, 0:SPAN], 1)
        load(pk.at[:, cols(a, core)], kbuf.at[a, 0:SPAN], 2)
    load(sk, skb, 3)
    load(sv, svb, 4)

    pltpu.make_async_copy(qraw, qraw, loc.at[0]).wait()
    qf = qraw[...].astype(F32)
    for j in range(16):
        qscr[2 * j : 2 * j + 2, :] = qf[:, D * j : D * (j + 1)]
    for k in range(2):
        qk = qscr[ROWS * k : ROWS * (k + 1), :].astype(BF)
        qz[z, k] = qk
        qc[c, k] = qk

    qbd[...] = jnp.zeros_like(qbd)
    fs[...] = jnp.zeros_like(fs)

    def turn(a, k, part):
        vt[a, k, 0:D, SPAN * part : SPAN * (part + 1)] = vbuf[
            a, SPAN * part : SPAN * (part + 1), D * k : D * (k + 1)
        ].T

    take(loc.at[1], 512)
    for a in range(2):
        for k in range(2):
            turn(a, k, 0)
            vt[a, k, D:TILE, :] = jnp.ones((16, 2 * SPAN), BF)

    pl.semaphore_wait(barrier, len(peers))

    for i in FAR:
        push(qz.at[z], qz.at[z], 0, rz1.at[0], zpeer(i))
    for i in range(1, 4):
        push(qz.at[z], qc.at[c], 1, rctx.at[0], cpeer(i))
    for a in range(2):
        push(pk.at[:, cols(a, 1 - core)], kbuf.at[a, SPAN : 2 * SPAN], 2, rkv.at[0], mate)
        push(pv.at[:, cols(a, 1 - core)], vbuf.at[a, SPAN : 2 * SPAN], 2, rkv.at[0], mate)

    take(rz1.at[0], 56)

    for i in ACROSS:
        push(qz.at[:, 0], q0.at[y, xlo, xhi], 3, rq2.at[i], ypeer(i))
        push(qz.at[:, 1], q1.at[x, y], 3, rq2.at[i], xpeer(i))
    q0[y, xlo, xhi] = qz[:, 0]
    q1[x, y] = qz[:, 1]

    def forward(j):
        t0 = q0.at[(y + NY - j) % NY, xlo, xhi]
        t1 = q1.at[(x + NX - j) % NX, y]
        for i in ACROSS:
            push(t0, t0, 4, rq3.at[0, j], xpeer(i))
            push(t1, t1, 4, rq3.at[1, j], ypeer(i))

    forward(0)

    take(rctx.at[0], 24)
    for h in range(8):
        qbd[ROWS * h : ROWS * (h + 1), D * h : D * (h + 1)] = qc[h // 2, h % 2]
    pltpu.make_async_copy(skb, skb, loc.at[3]).wait()
    pltpu.make_async_copy(svb, svb, loc.at[4]).wait()
    raw = jnp.concatenate([nt(qbd[...], skb[0]), nt(qbd[...], skb[1])], axis=1)
    row = lax.broadcasted_iota(jnp.int32, (8 * ROWS, 2 * SPAN), 0)
    col = lax.broadcasted_iota(jnp.int32, (8 * ROWS, 2 * SPAN), 1)
    branch = col // SPAN
    live = (row % 2 == branch) & (c * SPAN + col % SPAN < jnp.where(branch == 0, len_ref[0], len_ref[1]))
    raw = jnp.where(live, raw, NEG)
    stop = jnp.max(raw, axis=1, keepdims=True)
    w = jnp.where(live, jnp.exp2((raw - stop) * C2), 0.0).astype(BF)
    sden = jnp.sum(w.astype(F32), axis=1, keepdims=True)
    snum = jnp.dot(w[:, :SPAN], svb[0], preferred_element_type=F32) + jnp.dot(
        w[:, SPAN:], svb[1], preferred_element_type=F32
    )
    lane = lax.broadcasted_iota(jnp.int32, (8 * ROWS, D), 1)
    sstat = jnp.where(lane == 0, stop, sden)
    for h in range(8):
        r = slice(ROWS * (h % 2), ROWS * (h % 2) + ROWS)
        sb[h // 2, 0, r, :] = snum[ROWS * h : ROWS * (h + 1), D * h : D * (h + 1)]
        sb[h // 2, 1, r, :] = sstat[ROWS * h : ROWS * (h + 1), :]
    for i in range(1, 4):
        push(sb.at[(c + i) % 4], sr.at[i], 5, rsuf.at[0], cpeer(i))
    sr[0] = sb[c]

    for j in range(1, 4):
        take(rq2.at[j], 64)
        forward(j)

    take(loc.at[2], 512)
    take(rkv.at[0], 1024)
    for a in range(2):
        for k in range(2):
            turn(a, k, 1)

    def attend(units, after):
        def score(u, n):
            a, k, q = units[u][:3]
            rows = slice(CHUNK * n, CHUNK * (n + 1))
            s = nt(kbuf[a, rows, D * k : D * (k + 1)], q)
            ss[u % 2, rows] = s
            return jnp.max(s, axis=0, keepdims=True)

        count = 2 * SPAN // CHUNK
        tops = [score(0, n) for n in range(count)]
        for u, (a, k, _, out_a, out_b) in enumerate(units):
            top = functools.reduce(jnp.maximum, tops).astype(BF).astype(F32)
            tops = []
            for n in range(count):
                if u + 1 < len(units):
                    tops.append(score(u + 1, n))
                rows = slice(CHUNK * n, CHUNK * (n + 1))
                ps[u % 2, rows] = jnp.exp2((ss[u % 2, rows] - top) * C2).astype(BF)
            n = jnp.dot(vt[a, k], ps[u % 2], preferred_element_type=F32)
            den = n[D : D + 1, :]
            pack(out_a, n[0:D, :D], top[:, :D], den[:, :D])
            pack(out_b, n[0:D, D:], top[:, D:], den[:, D:])
            after(u)

    def partial(j, i):
        px = (x + i) % NX
        py = (y + i) % NY
        mine0 = o0.at[j, px % 2, px // 2]
        mine1 = o1.at[j, py]
        if isinstance(j, int) and j == LAST:
            to0, to1 = dev(px, (y + NY - j) % NY, z, core), dev((x + NX - j) % NX, py, z, core)
        else:
            to0, to1 = xpeer(i), ypeer(i)
        return (
            remote(mine0, rx0.at[i, j], sent.at[6], rp4.at[0, j], to0),
            remote(mine1, rx1.at[i, j], sent.at[6], rp4.at[1, j], to1),
        )

    def reduce(j):
        take(rp4.at[0, j], 108)
        pack(m0.at[j], *merge([o0.at[j, xlo, xhi]] + [rx0.at[i, j] for i in range(1, 4)]))
        take(rp4.at[1, j], 108)
        pack(m1.at[j], *merge([o1.at[j, y]] + [rx1.at[i, j] for i in range(1, 4)]))

    def step(j, _):
        py = (y + NY - j) % NY
        px = (x + NX - j) % NX
        take(rq3.at[0, j], 96)
        take(rq3.at[1, j], 96)
        units = [(a, 0, q0[py, a].reshape(256, D), o0.at[j, a, 0], o0.at[j, a, 1]) for a in range(2)]
        for v in range(2):
            q = q1[px, 2 * v : 2 * v + 2].reshape(256, D)
            units.append((px % 2, 1, q, o1.at[j, 2 * v], o1.at[j, 2 * v + 1]))

        order = (2, 1, 3, 0) if isinstance(j, int) else ACROSS

        def after(u):
            if u % 2:
                for i in order:
                    partial(j, i)[u // 2].start()

        attend(units, after)

        @pl.when(j > 0)
        def _():
            reduce(j - 1)

        @pl.when(j > 1)
        def _():
            push(m0.at[j - 1], ry0.at[j - 1], 7, rp5.at[0], ypeer(NY - j + 1))
            push(m1.at[j - 1], ry1.at[j - 1], 7, rp5.at[1], xpeer(NX - j + 1))

        return 0

    lax.fori_loop(0, LAST, step, 0)
    step(LAST, 0)
    take(rp5.at[0], 72)
    take(rp4.at[0, LAST], 144)
    n0, t0, d0 = merge([m0.at[0], ry0.at[1], ry0.at[2]] + [rx0.at[i, LAST] for i in range(4)])
    take(rp5.at[1], 72)
    take(rp4.at[1, LAST], 144)
    n1, t1, d1 = merge([m1.at[0], ry1.at[1], ry1.at[2]] + [rx1.at[i, LAST] for i in range(4)])

    zb[:, 0] = n0.T.astype(BF).reshape(NZ, ROWS, D)
    zb[:, 1] = n1.T.astype(BF).reshape(NZ, ROWS, D)
    h0 = d0.astype(BF).astype(F32)
    h1 = d1.astype(BF).astype(F32)
    srow = lax.broadcasted_iota(jnp.int32, (16, D), 0)
    st = jnp.zeros((16, D), F32)
    for n, v in enumerate((t0, h0, d0 - h0, t1, h1, d1 - h1)):
        st = jnp.where(srow == n, v, st)
    st = st.astype(BF)
    for i in range(NZ):
        zb[i, 2] = st
    for i in FAR:
        push(zb.at[(z + i) % NZ], rz.at[i], 8, rp6.at[0], zpeer(i))
    rz[0] = zb[z]

    take(rsuf.at[0], 96)
    suffix = []
    for k in range(2):
        r = slice(ROWS * k, ROWS * (k + 1))
        tops = [sr[i, 1, r, 0:1] for i in range(4)]
        top = jnp.maximum(jnp.maximum(tops[0], tops[1]), jnp.maximum(tops[2], tops[3]))
        num = jnp.zeros((ROWS, D), F32)
        den = jnp.zeros((ROWS, 1), F32)
        for i in range(4):
            f = jnp.exp2((tops[i] - top) * C2)
            num = num + f * sr[i, 0, r, :]
            den = den + f * sr[i, 1, r, 1:2]
        suffix.append((num, top, den))

    take(rp6.at[0], 84)
    stats = [rz[i, 2].astype(F32) for i in range(NZ)]
    for k in range(2):
        tops = [s[3 * k : 3 * k + 1, :] for s in stats]
        top = tops[0]
        for t in tops[1:]:
            top = jnp.maximum(top, t)
        den = jnp.zeros((1, D), F32)
        for i in range(NZ):
            f = jnp.exp2((tops[i] - top) * C2)
            den = den + f * (stats[i][3 * k + 1 : 3 * k + 2, :] + stats[i][3 * k + 2 : 3 * k + 3, :])
            fs[16 * k + i : 16 * k + i + 1, :] = f
        fs[16 * k + 8 : 16 * k + 9, :] = top
        fs[16 * k + 9 : 16 * k + 10, :] = den
    ft[...] = fs[...].T
    own = ft[pl.ds(pl.multiple_of(z * ROWS, ROWS), ROWS), :]
    for k in range(2):
        num = jnp.zeros((ROWS, D), F32)
        for i in range(NZ):
            num = num + own[:, 16 * k + i : 16 * k + i + 1] * rz[i, k].astype(F32)
        top = own[:, 16 * k + 8 : 16 * k + 9]
        den = own[:, 16 * k + 9 : 16 * k + 10]
        snum, stop, sden = suffix[k]
        both = jnp.maximum(top, stop)
        f = jnp.exp2((top - both) * C2)
        g = jnp.exp2((stop - both) * C2)
        att = (num * f + snum * g) / (den * f + sden * g)
        for j in range(8):
            oscr[:, D * (8 * k + j) : D * (8 * k + j + 1)] = att[2 * j : 2 * j + 2, :]
    out_ref[...] = oscr[...].astype(BF)

    for phase, kib in enumerate((56, 24, 1024, 192, 768, 96, 936, 144, 84)):
        take(sent.at[phase], kib)


def body(queries, prefix_keys, prefix_values, branch_suffix_keys, suffix_values, lengths):
    dma = pltpu.SemaphoreType.DMA
    vmem = pltpu.VMEM
    scratch = [
        vmem((2, 2048), BF),
        vmem((32, D), F32),
        vmem((NZ, 2, ROWS, D), BF),
        vmem((4, 2, ROWS, D), BF),
        vmem((NY, 2, 2, NZ, ROWS, D), BF),
        vmem((NX, NY, NZ, ROWS, D), BF),
        vmem((2, 2 * SPAN, 256), BF),
        vmem((2, 2 * SPAN, 256), BF),
        vmem((2, 2, TILE, 2 * SPAN), BF),
        vmem((2, SPAN, 1024), BF),
        vmem((2, SPAN, 1024), BF),
        vmem((128, 1024), BF),
        vmem((2, 2 * SPAN, 256), F32),
        vmem((2, 2 * SPAN, 256), BF),
        vmem((256, 8, D), F32),
        vmem((4, 2, 2, TILE, D), BF),
        vmem((4, NY, TILE, D), BF),
        vmem((4, 4, TILE, D), BF),
        vmem((4, 4, TILE, D), BF),
        vmem((4, TILE, D), BF),
        vmem((4, TILE, D), BF),
        vmem((4, TILE, D), BF),
        vmem((4, TILE, D), BF),
        vmem((NZ, 3, ROWS, D), BF),
        vmem((NZ, 3, ROWS, D), BF),
        vmem((4, 2, 32, D), F32),
        vmem((4, 2, 32, D), F32),
        vmem((D, D), F32),
        vmem((D, D), F32),
        vmem((2, 2048), F32),
        dma((9,)),
        dma((1,)),
        dma((4,)),
        dma((2, 4)),
        dma((2, 4)),
        dma((2,)),
        dma((1,)),
        dma((1,)),
        dma((1,)),
        dma((1,)),
        dma((5,)),
    ]
    hbm = pl.BlockSpec(memory_space=pltpu.HBM)
    return pl.pallas_call(
        kernel,
        out_shape=jax.ShapeDtypeStruct((2, 2048), BF),
        in_specs=[
            pl.BlockSpec(memory_space=pltpu.SMEM),
            hbm, hbm, hbm, hbm, hbm,
        ],
        out_specs=pl.BlockSpec(memory_space=pltpu.VMEM),
        scratch_shapes=scratch,
        compiler_params=pltpu.CompilerParams(
            collective_id=0, has_side_effects=True, vmem_limit_bytes=60 * 1024 * 1024
        ),
        cost_estimate=pl.CostEstimate(flops=2_800_000_000, bytes_accessed=8_000_000, transcendentals=4_500_000),
        name="attend",
    )(lengths, queries, prefix_keys, prefix_values, branch_suffix_keys, suffix_values)


def solution(mesh):
    placed = (
        P("br", "ctx"),
        P(("ctx", "br"), None),
        P(("ctx", "br"), None),
        P("br", "ctx", None),
        P("br", "ctx", None),
        P("br"),
    )
    return jax.shard_map(
        body, mesh=mesh, in_specs=placed, out_specs=P("br", "ctx"), check_vma=False
    )
```

profile of v0, /device:TPU:32, one launch (start us, length us, event | category | flops | bytes accessed | tf_op | source)
XLA Modules:
  0.0 44.0 jit_solution(11621751229276356886)
XLA Ops:
  0.0 42.7 %attend.1 = bf16[2,2048]{1,0:T(2,128)(2,1)} custom-call(s32[2]{0:T(128)} %len_ref.1, bf16[2,2048]{1,0:T(2,128)(2,1)} %q_ref.1, bf16[512,1024]{1,0:T(8,128)(2,1)} %pk.1, bf16[512,1024]{1,0:T(8,128)(2,1)} %pv.1, bf16[2,512,1024]{2,1,0:T(8,128)(2,1)} %sk.1, bf16[2,512,1024]{2,1,0:T(8,128)(2,1)} %sv.1), custom_call_target="tpu_custom_call" | custom-call | flops 2800000000 | bytes 8000000 | tf_op jit(solution)/shard_map/attend/pallas_call | solution.py:402
  42.7 1.3 %copy.8 = bf16[2,2048]{1,0:T(2,128)(2,1)} copy(bf16[2,2048]{1,0:T(2,128)(2,1)} %attend.1) | data formatting | bytes 16384
where the time goes:
time: 44.5 us; the launch traced here: 44 us
  Pallas kernels  42.7 us (96%)
  local copies, waits for them, and re-layouts  1.3 us (3%)
    pallas_call x1, Pallas kernels, body(): pl.pallas_call(kernel, out_shape=jax.ShapeDtypeStruct((2, 2048), BF), in_...  42.7 us
    unnamed x1, local copies, waits for them, and re-layouts  1.3 us

commit v1 on v0

--- a/solution.py
+++ b/solution.py
@@ -191,10 +191,6 @@
         r = slice(ROWS * (h % 2), ROWS * (h % 2) + ROWS)
         sb[h // 2, 0, r, :] = snum[ROWS * h : ROWS * (h + 1), D * h : D * (h + 1)]
         sb[h // 2, 1, r, :] = sstat[ROWS * h : ROWS * (h + 1), :]
-    for i in range(1, 4):
-        push(sb.at[(c + i) % 4], sr.at[i], 5, rsuf.at[0], cpeer(i))
-    sr[0] = sb[c]
-
     for j in range(1, 4):
         take(rq2.at[j], 64)
         forward(j)
@@ -281,6 +277,10 @@
 
     lax.fori_loop(0, LAST, step, 0)
     step(LAST, 0)
+    for i in range(1, 4):
+        push(sb.at[(c + i) % 4], sr.at[i], 5, rsuf.at[0], cpeer(i))
+    sr[0] = sb[c]
+
     take(rp5.at[0], 72)
     take(rp4.at[0, LAST], 144)
     n0, t0, d0 = merge([m0.at[0], ry0.at[1], ry0.at[2]] + [rx0.at[i, LAST] for i in range(4)])

time: 44.5 us -> 44.1 us (level)
  no operation moved by 1% of the time
where the time goes in v1:
time: 44.1 us; the launch traced here: 43.9 us
  Pallas kernels  42.6 us (97%)
  local copies, waits for them, and re-layouts  1.3 us (3%)
    pallas_call x1, Pallas kernels, body(): pl.pallas_call(kernel, out_shape=jax.ShapeDtypeStruct((2, 2048), BF), in_...  42.6 us
    unnamed x1, local copies, waits for them, and re-layouts  1.3 us

profile of v1, /device:TPU:32, one launch (start us, length us, event | category | flops | bytes accessed | tf_op | source)
XLA Modules:
  0.0 43.9 jit_solution(17310512738655101506)
XLA Ops:
  0.0 42.6 %attend.1 = bf16[2,2048]{1,0:T(2,128)(2,1)} custom-call(s32[2]{0:T(128)} %len_ref.1, bf16[2,2048]{1,0:T(2,128)(2,1)} %q_ref.1, bf16[512,1024]{1,0:T(8,128)(2,1)} %pk.1, bf16[512,1024]{1,0:T(8,128)(2,1)} %pv.1, bf16[2,512,1024]{2,1,0:T(8,128)(2,1)} %sk.1, bf16[2,512,1024]{2,1,0:T(8,128)(2,1)} %sv.1), custom_call_target="tpu_custom_call" | custom-call | flops 2800000000 | bytes 8000000 | tf_op jit(solution)/shard_map/attend/pallas_call | solution.py:402
  42.6 1.3 %copy.8 = bf16[2,2048]{1,0:T(2,128)(2,1)} copy(bf16[2,2048]{1,0:T(2,128)(2,1)} %attend.1) | data formatting | bytes 16384

commit v2 on v1

--- a/solution.py
+++ b/solution.py
@@ -143,30 +143,34 @@
 
     pl.semaphore_wait(barrier, len(peers))
 
+    for a in range(2):
+        push(pk.at[:, cols(a, 1 - core)], kbuf.at[a, SPAN : 2 * SPAN], 2, rkv.at[0], mate)
+        push(pv.at[:, cols(a, 1 - core)], vbuf.at[a, SPAN : 2 * SPAN], 2, rkv.at[0], mate)
     for i in FAR:
         push(qz.at[z], qz.at[z], 0, rz1.at[0], zpeer(i))
     for i in range(1, 4):
         push(qz.at[z], qc.at[c], 1, rctx.at[0], cpeer(i))
-    for a in range(2):
-        push(pk.at[:, cols(a, 1 - core)], kbuf.at[a, SPAN : 2 * SPAN], 2, rkv.at[0], mate)
-        push(pv.at[:, cols(a, 1 - core)], vbuf.at[a, SPAN : 2 * SPAN], 2, rkv.at[0], mate)
 
     take(rz1.at[0], 56)
 
     for i in ACROSS:
-        push(qz.at[:, 0], q0.at[y, xlo, xhi], 3, rq2.at[i], ypeer(i))
-        push(qz.at[:, 1], q1.at[x, y], 3, rq2.at[i], xpeer(i))
+        push(qz.at[:, 0], q0.at[y, xlo, xhi], 3, rq2.at[0, i], ypeer(i))
+        push(qz.at[:, 1], q1.at[x, y], 3, rq2.at[1, i], xpeer(i))
     q0[y, xlo, xhi] = qz[:, 0]
     q1[x, y] = qz[:, 1]
 
-    def forward(j):
-        t0 = q0.at[(y + NY - j) % NY, xlo, xhi]
-        t1 = q1.at[(x + NX - j) % NX, y]
+    def forward0(j):
+        part = q0.at[(y + NY - j) % NY, xlo, xhi]
         for i in ACROSS:
-            push(t0, t0, 4, rq3.at[0, j], xpeer(i))
-            push(t1, t1, 4, rq3.at[1, j], ypeer(i))
-
-    forward(0)
+            push(part, part, 4, rq3.at[0, j], xpeer(i))
+
+    def forward1(j):
+        part = q1.at[(x + NX - j) % NX, y]
+        for i in ACROSS:
+            push(part, part, 4, rq3.at[1, j], ypeer(i))
+
+    forward0(0)
+    forward1(0)
 
     take(rctx.at[0], 24)
     for h in range(8):
@@ -192,8 +196,10 @@
         sb[h // 2, 0, r, :] = snum[ROWS * h : ROWS * (h + 1), D * h : D * (h + 1)]
         sb[h // 2, 1, r, :] = sstat[ROWS * h : ROWS * (h + 1), :]
     for j in range(1, 4):
-        take(rq2.at[j], 64)
-        forward(j)
+        take(rq2.at[0, j], 32)
+        forward0(j)
+        take(rq2.at[1, j], 32)
+        forward1(j)
 
     take(loc.at[2], 512)
     take(rkv.at[0], 1024)
@@ -242,8 +248,18 @@
     def reduce(j):
         take(rp4.at[0, j], 108)
         pack(m0.at[j], *merge([o0.at[j, xlo, xhi]] + [rx0.at[i, j] for i in range(1, 4)]))
+        onward = j > 0
+
+        @pl.when(onward)
+        def _():
+            push(m0.at[j], ry0.at[j], 7, rp5.at[0], ypeer(NY - j))
+
         take(rp4.at[1, j], 108)
         pack(m1.at[j], *merge([o1.at[j, y]] + [rx1.at[i, j] for i in range(1, 4)]))
+
+        @pl.when(onward)
+        def _():
+            push(m1.at[j], ry1.at[j], 7, rp5.at[1], xpeer(NX - j))
 
     def step(j, _):
         py = (y + NY - j) % NY
@@ -267,11 +283,6 @@
         @pl.when(j > 0)
         def _():
             reduce(j - 1)
-
-        @pl.when(j > 1)
-        def _():
-            push(m0.at[j - 1], ry0.at[j - 1], 7, rp5.at[0], ypeer(NY - j + 1))
-            push(m1.at[j - 1], ry1.at[j - 1], 7, rp5.at[1], xpeer(NX - j + 1))
 
         return 0
 
@@ -388,7 +399,7 @@
         vmem((2, 2048), F32),
         dma((9,)),
         dma((1,)),
-        dma((4,)),
+        dma((2, 4)),
         dma((2, 4)),
         dma((2, 4)),
         dma((2,)),

time: 44.1 us -> 44.1 us (level)
  no operation moved by 1% of the time
where the time goes in v2:
time: 44.1 us; the launch traced here: 43.7 us
  Pallas kernels  42.4 us (96%)
  local copies, waits for them, and re-layouts  1.3 us (3%)
    pallas_call x1, Pallas kernels, body(): pl.pallas_call(kernel, out_shape=jax.ShapeDtypeStruct((2, 2048), BF), in_...  42.4 us
    unnamed x1, local copies, waits for them, and re-layouts  1.3 us

profile of v2, /device:TPU:32, one launch (start us, length us, event | category | flops | bytes accessed | tf_op | source)
XLA Modules:
  0.0 43.7 jit_solution(12140777456874912550)
XLA Ops:
  0.0 42.4 %attend.1 = bf16[2,2048]{1,0:T(2,128)(2,1)} custom-call(s32[2]{0:T(128)} %len_ref.1, bf16[2,2048]{1,0:T(2,128)(2,1)} %q_ref.1, bf16[512,1024]{1,0:T(8,128)(2,1)} %pk.1, bf16[512,1024]{1,0:T(8,128)(2,1)} %pv.1, bf16[2,512,1024]{2,1,0:T(8,128)(2,1)} %sk.1, bf16[2,512,1024]{2,1,0:T(8,128)(2,1)} %sv.1), custom_call_target="tpu_custom_call" | custom-call | flops 2800000000 | bytes 8000000 | tf_op jit(solution)/shard_map/attend/pallas_call | solution.py:413
  42.4 1.3 %copy.8 = bf16[2,2048]{1,0:T(2,128)(2,1)} copy(bf16[2,2048]{1,0:T(2,128)(2,1)} %attend.1) | data formatting | bytes 16384
